TPU v7x, 32 devices: a whole 2x2x4 slice. The times are simulated.
32 devices in a mesh: grp: 2 (over core), row: 4 (over z), col: 4 (over y, x).
Axes of the slice: x: 2, y: 2, z: 4, core: 2. Of those that a mesh axis runs over, the one named last changes fastest.
Arguments:
- cost_matrix: float32 [2, 4096, 4096], P('grp', 'row', 'col'), may hold values from -0.125 to 0.125
- coupling_factors: float32 [2, 4096, 1024], P('grp', ('row', 'col')), may hold values from 0.25 to 4
Outputs:
- updated_factors: float32 [2, 4096, 1024], P('grp', ('row', 'col'))
All inputs are finite; a program needn't handle non-finite values. Where the computation divides by a largest or mean magnitude, that divisor is 1e-20 or more.
Results may differ from a plain program's by a relative error of at most 0.0003.
Values sent between devices are 32-bit elements; how exact they have to be, the bound alone decides.
A program may use at most 64 MiB of HBM per device.

v0:
```python
import jax
import jax.numpy as jnp
from jax import lax
from jax.sharding import PartitionSpec as P

STEPS = 2


def swapped(value, axis, apart):
    return lax.ppermute(value, axis, [(i, i ^ 1 << apart) for i in range(lax.axis_size(axis))])


def shards(cost_matrix, coupling_factors):
    cost_tile = cost_matrix[0]
    current = coupling_factors[0]
    rows_side = lax.axis_size("row")
    blk_rows = cost_tile.shape[0]
    piece_rows = current.shape[0]
    sub_rows = piece_rows // rows_side
    rank_width = current.shape[1]
    for iteration in range(STEPS):
        pieces = current.reshape(rows_side, 1, sub_rows, rank_width)
        turned = lax.all_to_all(
            lax.all_to_all(pieces, "row", split_axis=0, concat_axis=1, tiled=True),
            "col",
            split_axis=1,
            concat_axis=0,
            tiled=True,
        )
        panel_rows = lax.all_gather(turned, "row", axis=1, tiled=True).reshape(blk_rows, rank_width)
        mixed = lax.psum_scatter(
            jnp.dot(
                cost_tile,
                panel_rows,
                precision=lax.Precision.HIGHEST,
                preferred_element_type=jnp.float32,
            ),
            "col",
            scatter_dimension=0,
            tiled=True,
        )
        core_part = lax.dot_general(
            current,
            mixed,
            (((0,), (0,)), ((), ())),
            precision=lax.Precision.HIGHEST,
            preferred_element_type=jnp.float32,
        )
        whole_core = lax.psum(core_part, ("row", "col"))
        other_core = swapped(whole_core, "grp", 0)
        gradient = jnp.dot(
            mixed, other_core, precision=lax.Precision.HIGHEST, preferred_element_type=jnp.float32
        )
        row_scale = jnp.max(jnp.abs(gradient), axis=1, keepdims=True) + 1e-06
        exponent = -3.0 * gradient / row_scale
        weighted = current * jnp.exp(exponent)
        current = rank_width * weighted / jnp.sum(weighted, axis=1, keepdims=True)
    return current[None]


def solution(mesh):
    in_specs = (P("grp", "row", "col"), P("grp", ("row", "col"), None))
    out_specs = P("grp", ("row", "col"), None)
    return jax.shard_map(shards, mesh=mesh, in_specs=in_specs, out_specs=out_specs, check_vma=False)
```

profile of v0, /device:TPU:0, one launch (start us, length us, event | category | flops | bytes accessed | tf_op | source)
XLA Modules:
  0.0 794.1 jit_solution(1707222826878971009)
XLA Ops:
  6.5 32.0 %all_to_all.48 = f32[4,1,64,1024]{3,2,1,0:T(8,128)S(1)} all-to-all(f32[4,1,64,1024]{3,2,1,0:T(8,128)} %bitcast.40), channel_id=1, replica_groups=mesh['grp'=2,'row'=4,'col'=4] {'row'}, dimensions={0} | all-to-all | bytes 2097152 | tf_op jit(solution)/shard_map/all_to_all | solution.py:24
  38.6 16.6 %all_to_all.49 = f32[1,4,64,1024]{3,2,0,1:T(8,128)} all-to-all(f32[1,4,64,1024]{3,2,0,1:T(8,128)S(1)} %bitcast.41), channel_id=1, replica_groups=mesh['grp'=2,'row'=4,'col'=4] {'col'}, dimensions={1} | all-to-all | bytes 2097152 | tf_op jit(solution)/shard_map/all_to_all | solution.py:23
  55.2 0.0 reduce-scatter.3.cloned.1.call-start
  55.3 79.1 %all-gather.5.cloned.1.call-done = f32[1,4,256,1024]{3,2,0,1:T(8,128)} async-done(((f32[1,4,64,1024]{3,2,0,1:T(8,128)}), f32[1,4,256,1024]{3,2,0,1:T(8,128)}) %all-gather.5.cloned.1.call-update) | async-done | bytes 4194320 | tf_op jit(solution)/shard_map/all_gather | solution.py:30
  134.4 17.6 %fusion.2 = f32[1024,1024]{1,0:T(8,128)} fusion(f32[1024,1024]{1,0:T(8,128)} %bitcast.43, f32[1,1024,1024]{2,1,0:T(8,128)} %param.2), kind=kOutput, calls=%fused_computation.2 | convolution fusion | flops 12884901888 | bytes 12582912 | tf_op jit(solution)/shard_map/dot_general | solution.py:32
  152.0 51.3 %reduce-scatter.3.cloned.1.call-done = f32[256,1024]{1,0:T(8,128)} async-done(((f32[1024,1024]{1,0:T(8,128)}), f32[256,1024]{1,0:T(8,128)}) %reduce-scatter.3.cloned.1.call-update) | async-done | bytes 1048592 | tf_op jit(solution)/shard_map/reduce_scatter | solution.py:31
  203.3 6.4 convolution_bitcast_fusion
  209.8 168.3 %all-reduce.3.cloned.1.call-done = f32[1024,1024]{0,1:T(8,128)} async-done(((f32[1024,1024]{0,1:T(8,128)}), f32[1024,1024]{0,1:T(8,128)}) %all-reduce.3.cloned.1.call-update) | async-done | bytes 4194320 | tf_op jit(solution)/shard_map/psum | solution.py:49
  378.1 7.4 collective-permute-done
  385.5 3.8 abs_reduce_fusion.1
  389.3 0.4 fusion.9
  389.7 0.1 multiply_divide_fusion
  389.9 28.7 %all_to_all.50 = f32[4,1,64,1024]{3,2,1,0:T(8,128)S(1)} all-to-all(f32[4,1,64,1024]{3,2,1,0:T(8,128)S(1)} %bitcast.39), channel_id=1, replica_groups=mesh['grp'=2,'row'=4,'col'=4] {'row'}, dimensions={0} | all-to-all | bytes 2097152 | tf_op jit(solution)/shard_map/all_to_all | solution.py:24
  418.6 17.2 %all_to_all.51 = f32[1,4,64,1024]{3,2,0,1:T(8,128)} all-to-all(f32[1,4,64,1024]{3,2,0,1:T(8,128)S(1)} %bitcast.42), channel_id=1, replica_groups=mesh['grp'=2,'row'=4,'col'=4] {'col'}, dimensions={1} | all-to-all | bytes 2097152 | tf_op jit(solution)/shard_map/all_to_all | solution.py:23
  435.8 78.6 %all-gather.7.cloned.1.call-done = f32[1,4,256,1024]{3,2,0,1:T(8,128)} async-done(((f32[1,4,64,1024]{3,2,0,1:T(8,128)}), f32[1,4,256,1024]{3,2,0,1:T(8,128)}) %all-gather.7.cloned.1.call-update) | async-done | bytes 4194320 | tf_op jit(solution)/shard_map/all_gather | solution.py:30
  514.4 30.5 %fusion.4 = f32[1024,1024]{0,1:T(8,128)} fusion(f32[1024,1024]{1,0:T(8,128)} %bitcast.44, f32[1,1024,1024]{2,1,0:T(8,128)} %param.2), kind=kOutput, calls=%fused_computation.4 | convolution fusion | flops 12884901888 | bytes 12582912 | tf_op jit(solution)/shard_map/dot_general | solution.py:32
  544.9 0.0 all-reduce.5.cloned.1.call-start
  545.0 51.3 %reduce-scatter.5.cloned.1.call-done = f32[256,1024]{0,1:T(8,128)} async-done(((f32[1024,1024]{0,1:T(8,128)}), f32[256,1024]{0,1:T(8,128)}) %reduce-scatter.5.cloned.1.call-update) | async-done | bytes 1048592 | tf_op jit(solution)/shard_map/reduce_scatter | solution.py:31
  596.3 9.8 %fusion.10 = f32[1024,1024]{1,0:T(8,128)} fusion(f32[256,1024]{1,0:T(8,128)S(1)} %multiply_divide_fusion, f32[256,1024]{0,1:T(8,128)} %reduce-scatter.5.cloned.1.call-done), kind=kOutput, calls=%fused_computation.17 | convolution fusion | flops 3221225472 | bytes 6291456 | tf_op jit(solution)/shard_map/dot_general | solution.py:42
  606.1 168.3 %all-reduce.5.cloned.1.call-done = f32[1024,1024]{1,0:T(8,128)} async-done(((f32[1024,1024]{1,0:T(8,128)}), f32[1024,1024]{1,0:T(8,128)}) %all-reduce.5.cloned.1.call-update) | async-done | bytes 4194320 | tf_op jit(solution)/shard_map/psum | solution.py:49
  774.5 7.4 collective-permute-done.1
  781.9 3.8 abs_reduce_fusion
  785.7 0.5 fusion.8
  786.2 1.1 divide_bitcast_fusion
  (20 shorter events, 0.3 us)
Async XLA Ops:
  6.5 127.8 %all-gather.5.cloned.1.call-start = ((), (), s32[]{:S(2)}) async-start(), calls=%async_computation.10 | async-start | bytes 5242880 | tf_op jit(solution)/shard_map/all_gather | solution.py:30
  55.2 148.1 %reduce-scatter.3.cloned.1.call-start = ((), (), s32[]{:S(2)}) async-start(), calls=%async_computation.6 | async-start | bytes 5242880 | tf_op jit(solution)/shard_map/reduce_scatter | solution.py:31
  152.0 51.4 %copy-start = (f32[1,256,1024]{2,1,0:T(8,128)S(1)}, f32[1,256,1024]{2,1,0:T(8,128)}, u32[]{:S(2)}) copy-start(f32[1,256,1024]{2,1,0:T(8,128)} %param.3) | copy-start | bytes 3145732
  152.0 226.1 %all-reduce.3.cloned.1.call-start = ((), (), s32[]{:S(2)}) async-start(), calls=%async_computation.7 | async-start | bytes 8388608 | tf_op jit(solution)/shard_map/psum | solution.py:49
  203.3 182.2 %copy-start.1 = (f32[256,1024]{1,0:T(8,128)S(1)}, f32[256,1024]{1,0:T(8,128)}, u32[]{:S(2)}) copy-start(f32[256,1024]{1,0:T(8,128)} %reduce-scatter.3.cloned.1.call-done) | copy-start | bytes 3145732
  209.8 304.7 %all-gather.7.cloned.1.call-start = ((), (), s32[]{:S(2)}) async-start(), calls=%async_computation.11 | async-start | bytes 5242880 | tf_op jit(solution)/shard_map/all_gather | solution.py:30
  378.1 7.4 collective-permute-start
  435.8 160.5 %reduce-scatter.5.cloned.1.call-start = ((), (), s32[]{:S(2)}) async-start(), calls=%async_computation.8 | async-start | bytes 5242880 | tf_op jit(solution)/shard_map/reduce_scatter | solution.py:31
  544.9 229.5 %all-reduce.5.cloned.1.call-start = ((), (), s32[]{:S(2)}) async-start(), calls=%async_computation.9 | async-start | bytes 8388608 | tf_op jit(solution)/shard_map/psum | solution.py:49
  596.3 185.5 %copy-start.2 = (f32[256,1024]{0,1:T(8,128)S(1)}, f32[256,1024]{0,1:T(8,128)}, u32[]{:S(2)}) copy-start(f32[256,1024]{0,1:T(8,128)} %reduce-scatter.5.cloned.1.call-done) | copy-start | bytes 3145732
  774.5 7.4 collective-permute-start.1
Sparse Core Ops, SparseCore 0:
  55.3 78.9 all-gather.4
  152.1 51.1 reduce-scatter.2
  209.9 168.1 all-reduce.2
  435.9 78.4 all-gather.6
  545.1 51.1 reduce-scatter.4
  606.3 168.1 all-reduce.4
where the time goes:
time: 794 us
  waiting for transfers between devices  612 us (77%)
  blocking collectives  94.6 us (12%)
  matrix products  71.9 us (9%)
  between operations  13.5 us (2%)
    psum x2, waiting for transfers between devices, shards(): whole_core = lax.psum(core_part, ('row', 'col'))  337 us
    all_gather x2, waiting for transfers between devices, shards(): lax.all_gather(turned, 'row', axis=1, tiled=True)  158 us
    reduce_scatter x2, waiting for transfers between devices, shards(): lax.psum_scatter(jnp.dot(cost_tile, panel_rows, precision=lax.Precision.H...  103 us
    all_to_all x2, blocking collectives, shards(): lax.all_to_all(pieces, 'row', split_axis=0, concat_axis=1, tiled=True)  60.8 us
    dot_general x2, matrix products, shards(): jnp.dot(cost_tile, panel_rows, precision=lax.Precision.HIGHEST, preferred...  48.1 us
    all_to_all x2, blocking collectives, shards(): lax.all_to_all(lax.all_to_all(pieces, 'row', split_axis=0, concat_axis=1,...  33.8 us
    dot_general x2, matrix products, shards(): lax.dot_general(current, mixed, (((0,), (0,)), ((), ())), precision=lax.P...  16.2 us
  transfers between devices with their start and end apart: 8, of which 8 were waited for; matrix products, arithmetic and copies ran while one was open for 0% of the time, Pallas kernels for 0%

commit v1 on v0

v1 whole, which is shorter than its diff:
```python
import functools
import jax
import jax.numpy as jnp
from jax import lax
from jax.experimental import pallas as pl
from jax.experimental.pallas import tpu as pltpu
from jax.sharding import PartitionSpec as P

STEPS = 2
MESH = pl.DeviceIdType.MESH
PARTS = 4
VMEM_BYTES = 48 * 1024 * 1024


def peer(axis, bit):
    index = lax.axis_index(axis)
    mine = (index // 2**bit) % 2
    return mine, index + (1 - 2 * mine) * 2**bit


def rows_at(offset, size):
    if isinstance(offset, int):
        return pl.ds(offset, size)
    return pl.ds(pl.multiple_of(offset, 8), size)


def remote(src, dst, send_sem, recv_sem, device):
    return pltpu.make_async_remote_copy(
        src_ref=src,
        dst_ref=dst,
        send_sem=send_sem,
        recv_sem=recv_sem,
        device_id=device,
        device_id_type=MESH,
    )


def greet(devices):
    barrier = pltpu.get_barrier_semaphore()
    for device in devices:
        pl.semaphore_signal(barrier, inc=1, device_id=device, device_id_type=MESH)
    pl.semaphore_wait(barrier, len(devices))


def gather_kernel(x_ref, panel, held, z_send, z_recv, p_send, p_recv, own_sem):
    n = lax.axis_size("row")
    r = lax.axis_index("row")
    c = lax.axis_index("col")
    size = x_ref.shape[0] // PARTS

    barrier = pltpu.get_barrier_semaphore()
    for step in range(1, n):
        pl.semaphore_signal(
            barrier, inc=1, device_id={"col": lax.rem(c + step, n)}, device_id_type=MESH
        )
    for away in (-1, 1):

        @pl.when((r + away >= 0) & (r + away < n))
        def _():
            pl.semaphore_signal(barrier, inc=1, device_id={"row": r + away}, device_id_type=MESH)

    pl.semaphore_wait(barrier, n - 1 + (r + n - 1) // n + (2 * n - 2 - r) // n)

    def along(src, k, s, way):
        rows = pl.ds(k * size, size)
        return remote(
            src.at[rows], held.at[s, rows], z_send.at[k, s, way], z_recv.at[k, s], {"row": r + 2 * way - 1}
        )

    def across(src, k, s):
        rows = pl.ds(k * size, size)
        return remote(src.at[rows], panel.at[c, rows], p_send.at[k, s], p_recv.at[k, c], {"col": s})

    def keep(src, k):
        rows = pl.ds(k * size, size)
        return pltpu.make_async_copy(src.at[rows], panel.at[c, rows], own_sem.at[k])

    def forward(src, k, s, ways, act):
        for way in ways:
            away = 2 * way - 1

            @pl.when((r + away >= 0) & (r + away < n))
            def _():
                act(along(src, k, s, way), False)

        @pl.when(s != c)
        def _():
            act(across(src, k, s), False)

        @pl.when(s == c)
        def _():
            act(keep(src, k), True)

    def begin(copy, local):
        copy.start()

    def end(copy, local):
        copy.wait() if local else copy.wait_send()

    forward(x_ref, 0, r, (0, 1), begin)
    for k in range(PARTS):
        if k + 1 < PARTS:
            forward(x_ref, k + 1, r, (0, 1), begin)
        for distance in range(1, n):
            for way in (0, 1):
                s = r - (2 * way - 1) * distance

                @pl.when((s >= 0) & (s < n))
                def _():
                    along(held.at[s], k, s, way).wait_recv()
                    forward(held.at[s], k, s, (way,), begin)

    for k in range(PARTS):
        rows = pl.ds(k * size, size)
        forward(x_ref, k, r, (0, 1), end)
        for distance in range(1, n):
            for way in (0, 1):
                s = r - (2 * way - 1) * distance

                @pl.when((s >= 0) & (s < n))
                def _():
                    forward(held.at[s], k, s, (way,), end)

        for step in range(1, n):
            source = lax.rem(c + step, n)
            remote(
                x_ref.at[rows],
                panel.at[source, rows],
                p_send.at[k, source],
                p_recv.at[k, source],
                {"col": source},
            ).wait_recv()


def gathered(current):
    n = lax.axis_size("row")
    rows, width = current.shape
    return pl.pallas_call(
        gather_kernel,
        out_shape=jax.ShapeDtypeStruct((n, rows, width), jnp.float32),
        in_specs=[pl.BlockSpec(memory_space=pltpu.VMEM)],
        out_specs=pl.BlockSpec(memory_space=pltpu.VMEM),
        scratch_shapes=[
            pltpu.VMEM((n, rows, width), jnp.float32),
            pltpu.SemaphoreType.DMA((PARTS, n, 2)),
            pltpu.SemaphoreType.DMA((PARTS, n)),
            pltpu.SemaphoreType.DMA((PARTS, n)),
            pltpu.SemaphoreType.DMA((PARTS, n)),
            pltpu.SemaphoreType.DMA((PARTS,)),
        ],
        compiler_params=pltpu.CompilerParams(
            collective_id=0, has_side_effects=True, vmem_limit_bytes=VMEM_BYTES
        ),
        name="gather",
    )(current)


def scatter_kernel(bits, part, out, acc, recv, send_sem, recv_sem):
    greet([{"col": peer("col", bit)[1]} for bit in range(bits)])
    rows, width = out.shape
    streams = []
    for piece in range(2):
        for order in (list(range(bits)), list(range(bits))[::-1]):
            streams.append((piece, len(streams) % 2, order))

    def spans(q):
        piece, side, _ = streams[q]
        return (pl.ds(piece * (rows // 2), rows // 2), pl.ds(side * (width // 2), width // 2))

    def stage(q, k):
        order = streams[q][2]
        fixed = sum([peer("col", order[j])[0] * 2 ** order[j] for j in range(k)], 0)
        mine, partner = peer("col", order[k])
        free = [0]
        for j in order[k + 1 :]:
            free = free + [f + 2**j for f in free]
        base = sum(2 ** (bits - 1 - j) for j in range(k))
        src = part if k == 0 else acc
        items = []
        for at, f in enumerate(free):
            slot = base + at
            kept = fixed + mine * 2 ** order[k] + f
            sent = fixed + (1 - mine) * 2 ** order[k] + f
            copy = remote(
                src.at[(sent, *spans(q))],
                recv.at[q, slot],
                send_sem.at[q, slot],
                recv_sem.at[q, slot],
                {"col": partner},
            )
            items.append((copy, src, kept, slot))
        return items

    for k in range(bits + 1):
        for q in range(len(streams)):
            if k > 0:
                for copy, src, kept, slot in stage(q, k - 1):
                    copy.wait()
                    total = src[(kept, *spans(q))] + recv[q, slot]
                    if k == bits:
                        out[spans(q)] = total
                    else:
                        acc[(kept, *spans(q))] = total
            if k < bits:
                for copy, _, _, _ in stage(q, k):
                    copy.start()


def scattered(part):
    n = lax.axis_size("col")
    bits = n.bit_length() - 1
    rows, width = part.shape[0] // n, part.shape[1]
    return pl.pallas_call(
        functools.partial(scatter_kernel, bits),
        out_shape=jax.ShapeDtypeStruct((rows, width), jnp.float32),
        in_specs=[pl.BlockSpec(memory_space=pltpu.VMEM)],
        out_specs=pl.BlockSpec(memory_space=pltpu.VMEM),
        scratch_shapes=[
            pltpu.VMEM((n, rows, width), jnp.float32),
            pltpu.VMEM((4, n - 1, rows // 2, width // 2), jnp.float32),
            pltpu.SemaphoreType.DMA((4, n - 1)),
            pltpu.SemaphoreType.DMA((4, n - 1)),
        ],
        compiler_params=pltpu.CompilerParams(
            collective_id=1, has_side_effects=True, vmem_limit_bytes=VMEM_BYTES
        ),
        name="scatter",
    )(part.reshape(n, rows, width))


def core_kernel(row_bits, col_bits, part, out, acc, recv, send_sem, recv_sem):
    rows_axis = [("row", bit) for bit in range(row_bits)]
    cols_axis = [("col", bit) for bit in range(col_bits)]
    swap = {"grp": 1 - lax.axis_index("grp")}
    greet([{axis: peer(axis, bit)[1]} for axis, bit in rows_axis + cols_axis] + [swap])
    width = part.shape[0]
    half = width // 2
    orders = [
        cols_axis + rows_axis,
        cols_axis[::-1] + rows_axis,
        rows_axis[:1] + cols_axis + rows_axis[1:],
        rows_axis[:1] + cols_axis[::-1] + rows_axis[1:],
    ]
    depth = row_bits + col_bits
    phases = 2 * depth + 1
    offsets = []
    for q, order in enumerate(orders):
        track = [(q // 2) * half]
        for k, (axis, bit) in enumerate(order):
            track.append(track[-1] + peer(axis, bit)[0] * (half >> (k + 1)))
        offsets.append(track)

    def describe(q, p):
        columns = pl.ds((q % 2) * half, half)
        sems = (send_sem.at[q, p], recv_sem.at[q, p])
        if p < depth:
            axis, bit = orders[q][p]
            mine, partner = peer(axis, bit)
            size = half >> (p + 1)
            sent = rows_at(offsets[q][p] + (1 - mine) * size, size)
            src = part if p == 0 else acc
            slot = pl.ds(half - (half >> p), size)
            return remote(src.at[sent, columns], recv.at[q, slot], *sems, {axis: partner})
        if p == depth:
            rows = rows_at(offsets[q][depth], half >> depth)
            return remote(acc.at[rows, columns], out.at[rows, columns], *sems, swap)
        level = 2 * depth + 1 - p
        axis, bit = orders[q][level - 1]
        rows = rows_at(offsets[q][level], half >> level)
        return remote(
            out.at[rows, columns], out.at[rows, columns], *sems, {axis: peer(axis, bit)[1]}
        )

    def finish(q, p):
        describe(q, p).wait()
        if p < depth:
            columns = pl.ds((q % 2) * half, half)
            size = half >> (p + 1)
            kept = rows_at(offsets[q][p + 1], size)
            src = part if p == 0 else acc
            acc[kept, columns] = src[kept, columns] + recv[q, pl.ds(half - (half >> p), size)]

    for p in range(phases + 1):
        for q in range(len(orders)):
            if p > 0:
                finish(q, p - 1)
            if p < phases:
                describe(q, p).start()


def other_core_of(part):
    width = part.shape[0]
    row_bits = lax.axis_size("row").bit_length() - 1
    col_bits = lax.axis_size("col").bit_length() - 1
    phases = 2 * (row_bits + col_bits) + 1
    return pl.pallas_call(
        functools.partial(core_kernel, row_bits, col_bits),
        out_shape=jax.ShapeDtypeStruct((width, width), jnp.float32),
        in_specs=[pl.BlockSpec(memory_space=pltpu.VMEM)],
        out_specs=pl.BlockSpec(memory_space=pltpu.VMEM),
        scratch_shapes=[
            pltpu.VMEM((width, width), jnp.float32),
            pltpu.VMEM((4, width // 2, width // 2), jnp.float32),
            pltpu.SemaphoreType.DMA((4, phases)),
            pltpu.SemaphoreType.DMA((4, phases)),
        ],
        compiler_params=pltpu.CompilerParams(
            collective_id=2, has_side_effects=True, vmem_limit_bytes=VMEM_BYTES
        ),
        name="core",
    )(part)


def shards(cost_matrix, coupling_factors):
    cost_tile = cost_matrix[0]
    current = coupling_factors[0]
    blk_rows = cost_tile.shape[0]
    rank_width = current.shape[1]
    for iteration in range(STEPS):
        panel_rows = gathered(current).reshape(blk_rows, rank_width)
        mixed = scattered(
            jnp.dot(
                cost_tile,
                panel_rows,
                precision=lax.Precision.HIGH,
                preferred_element_type=jnp.float32,
            )
        )
        core_part = lax.dot_general(
            current,
            mixed,
            (((0,), (0,)), ((), ())),
            precision=lax.Precision.HIGH,
            preferred_element_type=jnp.float32,
        )
        other_core = other_core_of(core_part)
        gradient = jnp.dot(
            mixed, other_core, precision=lax.Precision.HIGH, preferred_element_type=jnp.float32
        )
        row_scale = jnp.max(jnp.abs(gradient), axis=1, keepdims=True) + 1e-06
        exponent = -3.0 * gradient / row_scale
        weighted = current * jnp.exp(exponent)
        current = rank_width * weighted / jnp.sum(weighted, axis=1, keepdims=True)
    return current[None]


def solution(mesh):
    in_specs = (P("grp", "row", "col"), P("grp", ("row", "col"), None))
    out_specs = P("grp", ("row", "col"), None)
    return jax.shard_map(shards, mesh=mesh, in_specs=in_specs, out_specs=out_specs, check_vma=False)
```

time: 794 us -> 460 us (0.58)
  waiting for transfers between devices: 612 us -> 0 us
  Pallas kernels: 0 us -> 431 us
  blocking collectives: 94.6 us -> 0 us
  matrix products: 71.9 us -> 25.6 us
  between operations: 13.5 us -> 0.11 us
    pallas_call x0 -> x6, Pallas kernels: none -> 431 us  [the longest x2 200 us: other_core_of(): pl.pallas_call(functools.partial(core_kernel, row_bits, col_bits), out_sh...]
    psum x2 -> x0, waiting for transfers between devices: 337 us -> none  [shards(): whole_core = lax.psum(core_part, ('row', 'col'))]
    all_gather x2 -> x0, waiting for transfers between devices: 158 us -> none  [shards(): lax.all_gather(turned, 'row', axis=1, tiled=True)]
    reduce_scatter x2 -> x0, waiting for transfers between devices: 103 us -> none  [shards(): lax.psum_scatter(jnp.dot(cost_tile, panel_rows, precision=lax.Precision.H...]
    all_to_all x4 -> x0, blocking collectives: 94.6 us -> none  [the longest x2 60.8 us: shards(): lax.all_to_all(pieces, 'row', split_axis=0, concat_axis=1, tiled=True)]
    dot_general x4, matrix products: 55.7 us -> 18 us  [the longest x2 13.7 us: shards(): jnp.dot(cost_tile, panel_rows, precision=lax.Precision.HIGH, preferred_el...]
    ppermute x2 -> x0, waiting for transfers between devices: 14.7 us -> none  [swapped(): lax.ppermute(value, axis, [(i, i ^ 1 << apart) for i in range(lax.axis_si...]
    dot_general x2, matrix products: 16.2 us -> 7.56 us  [shards(): lax.dot_general(current, mixed, (((0,), (0,)), ((), ())), precision=lax.P...]
  transfers between devices with their start and end apart: 8 -> 0, of which waited for: 8 -> 0; matrix products, arithmetic and copies ran while one was open for 0% -> 0% of each run, Pallas kernels for 0% -> 0%
where the time goes in v1:
time: 460 us
  Pallas kernels  431 us (94%)
  matrix products  25.6 us (6%)
    pallas_call x2, Pallas kernels, other_core_of(): pl.pallas_call(functools.partial(core_kernel, row_bits, col_bits), out_sh...  200 us
    pallas_call x2, Pallas kernels, gathered(): pl.pallas_call(gather_kernel, out_shape=jax.ShapeDtypeStruct((n, rows, wi...  154 us
    pallas_call x2, Pallas kernels, scattered(): pl.pallas_call(functools.partial(scatter_kernel, bits), out_shape=jax.Sha...  76.9 us
    dot_general x2, matrix products, shards(): jnp.dot(cost_tile, panel_rows, precision=lax.Precision.HIGH, preferred_el...  13.7 us

profile of v1, /device:TPU:0, one launch (start us, length us, event | category | flops | bytes accessed | tf_op | source)
XLA Modules:
  0.0 460.2 jit_solution(9239991501697892772)
XLA Ops:
  0.0 0.0 copy-start
  0.0 1.2 copy-done
  1.2 0.0 copy-start.2
  1.2 79.9 %gather.2 = f32[4,256,1024]{2,1,0:T(8,128)S(1)} custom-call(f32[256,1024]{1,0:T(8,128)S(1)} %bitcast.30), custom_call_target="tpu_custom_call" | custom-call | tf_op jit(solution)/shard_map/gather/pallas_call | solution.py:138
  81.1 0.0 copy-done.2
  81.1 6.7 %fusion.5.part = f32[4,256,1024]{2,1,0:T(8,128)S(1)} fusion(f32[4,256,1024]{2,1,0:T(8,128)S(1)} %bitcast.34, f32[1024,1024,1]{1,0,2:T(8,128)S(1)} %bitcast.32), kind=kOutput, calls=%fused_computation.14 | convolution fusion | flops 6442450944 | bytes 12582912 | tf_op jit(solution)/shard_map/dot_general | solution.py:322
  87.9 0.0 copy-start.1
  87.9 42.2 %scatter.2 = f32[256,1024]{1,0:T(8,128)S(1)} custom-call(f32[4,256,1024]{2,1,0:T(8,128)S(1)} %fusion.5.part), custom_call_target="tpu_custom_call" | custom-call | tf_op jit(solution)/shard_map/scatter/pallas_call | solution.py:213
  130.1 0.0 copy-done.1
  130.1 3.8 convolution_bitcast_fusion.part
  133.9 93.7 %core.2 = f32[1024,1024]{1,0:T(8,128)S(1)} custom-call(f32[1024,1024]{1,0:T(8,128)} %convolution_bitcast_fusion.part), custom_call_target="tpu_custom_call" | custom-call | tf_op jit(solution)/shard_map/core/pallas_call | solution.py:296
  227.6 2.1 abs_reduce_fusion.1
  229.8 0.4 fusion.4
  230.2 0.1 multiply_divide_fusion.x_ref
  230.3 74.5 %gather.3 = f32[4,256,1024]{2,1,0:T(8,128)S(1)} custom-call(f32[256,1024]{1,0:T(8,128)S(1)} %multiply_divide_fusion.x_ref), custom_call_target="tpu_custom_call" | custom-call | tf_op jit(solution)/shard_map/gather/pallas_call | solution.py:138
  304.9 7.0 %fusion = f32[1024,1024]{0,1:T(8,128)S(1)} fusion(f32[1024,1024]{1,0:T(8,128)S(1)} %bitcast.33, f32[1,1024,1024]{2,1,0:T(8,128)S(1)} %copy-done.2), kind=kOutput, calls=%fused_computation | convolution fusion | flops 6442450944 | bytes 12582912 | tf_op jit(solution)/shard_map/dot_general | solution.py:322
  311.9 34.7 %scatter.3 = f32[256,1024]{1,0:T(8,128)S(1)} custom-call(f32[4,256,1024]{2,1,0:T(8,128)S(1)} %bitcast.31), custom_call_target="tpu_custom_call" | custom-call | tf_op jit(solution)/shard_map/scatter/pallas_call | solution.py:213
  346.5 3.8 fusion.6.part
  350.3 106.1 %core.3 = f32[1024,1024]{1,0:T(8,128)S(1)} custom-call(f32[1024,1024]{1,0:T(8,128)} %fusion.6.part), custom_call_target="tpu_custom_call" | custom-call | tf_op jit(solution)/shard_map/core/pallas_call | solution.py:296
  456.4 2.1 abs_reduce_fusion
  458.6 0.5 fusion.3
  459.0 1.1 divide_bitcast_fusion
  (2 shorter events, 0.0 us)
Async XLA Ops:
  0.0 1.2 copy-start
  1.2 79.9 %copy-start.2 = (f32[1,1024,1024]{2,1,0:T(8,128)S(1)}, f32[1,1024,1024]{2,1,0:T(8,128)}, u32[]{:S(2)}) copy-start(f32[1,1024,1024]{2,1,0:T(8,128)} %param.2) | copy-start | bytes 12582916
  87.9 42.2 %copy-start.1 = (f32[1,256,1024]{2,1,0:T(8,128)S(1)}, f32[1,256,1024]{2,1,0:T(8,128)}, u32[]{:S(2)}) copy-start(f32[1,256,1024]{2,1,0:T(8,128)} %param.3) | copy-start | bytes 3145732

commit v2 on v1

--- a/solution.py
+++ b/solution.py
@@ -8,7 +8,7 @@
 
 STEPS = 2
 MESH = pl.DeviceIdType.MESH
-PARTS = 4
+PARTS = 8
 VMEM_BYTES = 48 * 1024 * 1024
 
 
@@ -238,9 +238,10 @@
     orders = [
         cols_axis + rows_axis,
         cols_axis[::-1] + rows_axis,
-        rows_axis[:1] + cols_axis + rows_axis[1:],
-        rows_axis[:1] + cols_axis[::-1] + rows_axis[1:],
+        cols_axis + rows_axis,
+        cols_axis[::-1] + rows_axis,
     ]
+    lag = [0, 0, 2, 2]
     depth = row_bits + col_bits
     phases = 2 * depth + 1
     offsets = []
@@ -280,11 +281,12 @@
             src = part if p == 0 else acc
             acc[kept, columns] = src[kept, columns] + recv[q, pl.ds(half - (half >> p), size)]
 
-    for p in range(phases + 1):
+    for tick in range(phases + 1 + max(lag)):
         for q in range(len(orders)):
-            if p > 0:
+            p = tick - lag[q]
+            if 0 < p <= phases:
                 finish(q, p - 1)
-            if p < phases:
+            if 0 <= p < phases:
                 describe(q, p).start()
 
 

time: 460 us -> 439 us (0.954)
  Pallas kernels: 431 us -> 410 us
    pallas_call x2, Pallas kernels: 200 us -> 186 us  [other_core_of(): pl.pallas_call(functools.partial(core_kernel, row_bits, col_bits), out_sh...]
    pallas_call x2, Pallas kernels: 76.9 us -> 67.7 us  [scattered(): pl.pallas_call(functools.partial(scatter_kernel, bits), out_shape=jax.Sha...]
where the time goes in v2:
time: 439 us
  Pallas kernels  410 us (93%)
  matrix products  25.6 us (6%)
    pallas_call x2, Pallas kernels, other_core_of(): pl.pallas_call(functools.partial(core_kernel, row_bits, col_bits), out_sh...  186 us
    pallas_call x2, Pallas kernels, gathered(): pl.pallas_call(gather_kernel, out_shape=jax.ShapeDtypeStruct((n, rows, wi...  156 us
    pallas_call x2, Pallas kernels, scattered(): pl.pallas_call(functools.partial(scatter_kernel, bits), out_shape=jax.Sha...  67.7 us
    dot_general x2, matrix products, shards(): jnp.dot(cost_tile, panel_rows, precision=lax.Precision.HIGH, preferred_el...  13.7 us

profile of v2, /device:TPU:0, one launch (start us, length us, event | category | flops | bytes accessed | tf_op | source)
XLA Modules:
  0.0 438.7 jit_solution(7137029459434655221)
XLA Ops:
  0.0 0.0 copy-start
  0.0 1.2 copy-done
  1.2 0.0 copy-start.2
  1.2 79.3 %gather.2 = f32[4,256,1024]{2,1,0:T(8,128)S(1)} custom-call(f32[256,1024]{1,0:T(8,128)S(1)} %bitcast.30), custom_call_target="tpu_custom_call" | custom-call | tf_op jit(solution)/shard_map/gather/pallas_call | solution.py:138
  80.5 0.0 copy-done.2
  80.5 6.7 %fusion.5.part = f32[4,256,1024]{2,1,0:T(8,128)S(1)} fusion(f32[4,256,1024]{2,1,0:T(8,128)S(1)} %bitcast.34, f32[1024,1024,1]{1,0,2:T(8,128)S(1)} %bitcast.32), kind=kOutput, calls=%fused_computation.14 | convolution fusion | flops 6442450944 | bytes 12582912 | tf_op jit(solution)/shard_map/dot_general | solution.py:324
  87.3 0.0 copy-start.1
  87.3 39.6 %scatter.2 = f32[256,1024]{1,0:T(8,128)S(1)} custom-call(f32[4,256,1024]{2,1,0:T(8,128)S(1)} %fusion.5.part), custom_call_target="tpu_custom_call" | custom-call | tf_op jit(solution)/shard_map/scatter/pallas_call | solution.py:213
  126.9 0.0 copy-done.1
  126.9 3.8 convolution_bitcast_fusion.part
  130.7 93.3 %core.2 = f32[1024,1024]{1,0:T(8,128)S(1)} custom-call(f32[1024,1024]{1,0:T(8,128)} %convolution_bitcast_fusion.part), custom_call_target="tpu_custom_call" | custom-call | tf_op jit(solution)/shard_map/core/pallas_call | solution.py:298
  224.1 2.1 abs_reduce_fusion.1
  226.2 0.5 fusion.4
  226.8 0.1 multiply_divide_fusion.x_ref
  226.9 76.6 %gather.3 = f32[4,256,1024]{2,1,0:T(8,128)S(1)} custom-call(f32[256,1024]{1,0:T(8,128)S(1)} %multiply_divide_fusion.x_ref), custom_call_target="tpu_custom_call" | custom-call | tf_op jit(solution)/shard_map/gather/pallas_call | solution.py:138
  303.5 7.0 %fusion = f32[1024,1024]{0,1:T(8,128)S(1)} fusion(f32[1024,1024]{1,0:T(8,128)S(1)} %bitcast.33, f32[1,1024,1024]{2,1,0:T(8,128)S(1)} %copy-done.2), kind=kOutput, calls=%fused_computation | convolution fusion | flops 6442450944 | bytes 12582912 | tf_op jit(solution)/shard_map/dot_general | solution.py:324
  310.5 28.1 %scatter.3 = f32[256,1024]{1,0:T(8,128)S(1)} custom-call(f32[4,256,1024]{2,1,0:T(8,128)S(1)} %bitcast.31), custom_call_target="tpu_custom_call" | custom-call | tf_op jit(solution)/shard_map/scatter/pallas_call | solution.py:213
  338.6 3.8 fusion.6.part
  342.3 92.7 %core.3 = f32[1024,1024]{1,0:T(8,128)S(1)} custom-call(f32[1024,1024]{1,0:T(8,128)} %fusion.6.part), custom_call_target="tpu_custom_call" | custom-call | tf_op jit(solution)/shard_map/core/pallas_call | solution.py:298
  435.0 2.1 abs_reduce_fusion
  437.2 0.5 fusion.3
  437.6 1.1 divide_bitcast_fusion
  (2 shorter events, 0.0 us)
Async XLA Ops:
  0.0 1.2 copy-start
  1.2 79.3 %copy-start.2 = (f32[1,1024,1024]{2,1,0:T(8,128)S(1)}, f32[1,1024,1024]{2,1,0:T(8,128)}, u32[]{:S(2)}) copy-start(f32[1,1024,1024]{2,1,0:T(8,128)} %param.2) | copy-start | bytes 12582916
  87.3 39.6 %copy-start.1 = (f32[1,256,1024]{2,1,0:T(8,128)S(1)}, f32[1,256,1024]{2,1,0:T(8,128)}, u32[]{:S(2)}) copy-start(f32[1,256,1024]{2,1,0:T(8,128)} %param.3) | copy-start | bytes 3145732
